TPU v7x, 32 devices: a whole 2x2x4 slice. The times are simulated.
32 devices in a mesh: row: 4 (over x, core), col: 8 (over z, y).
Axes of the slice: x: 2, y: 2, z: 4, core: 2. Of those that a mesh axis runs over, the one named last changes fastest.
Arguments:
- features: bfloat16 [64, 128, 1024], P(None, 'row', 'col'), may hold values from -6 to 6
- patch_index: int32 [128, 1024], P('row', 'col'), may hold values from 0 to 2047
- confidence: float32 [128, 1024], P('row', 'col'), may hold values from 0.2 to 1
- bank: bfloat16 [32, 576, 2048], P(('row', 'col')), may hold values from -6 to 6
- page_owner: int32 [2], replicated, may hold values from 0 to 31
- texture_weight: bfloat16 [64, 576], replicated, may hold values from -0.25 to 0.25
- conv_weight: bfloat16 [8, 9, 64, 64], replicated, may hold values from -0.25 to 0.25
Outputs:
- restored: bfloat16 [64, 128, 1024], P(None, 'row', 'col')
Inputs may be any that keep to these rules, and one draw needn't show every extreme that they name: `patch_index`: each entry is a patch number of the page. `page_owner`: each entry is a slot number.
All inputs are finite; a program needn't handle non-finite values.
Results may differ from a plain program's by a relative error of at most 0.024.
Values may be sent and summed in bfloat16 or wider, within the bound.
A program may use at most 128 MiB of HBM per device.

v0:
```python
import jax
import jax.numpy as jnp
from jax import lax
from jax.sharding import PartitionSpec as P

LAYERS = 8
STEPS = 2


def with_halo(block, sides, width):
    for axis, dim in sides:
        count = lax.axis_size(axis)
        forward = [(i, i + 1) for i in range(count - 1)]
        backward = [(target, source) for source, target in forward]
        low = lax.ppermute(
            lax.slice_in_dim(block, block.shape[dim] - width, None, axis=dim), axis, forward
        )
        high = lax.ppermute(lax.slice_in_dim(block, 0, width, axis=dim), axis, backward)
        block = jnp.concatenate([low, block, high], axis=dim)
    return block


def broadcast(value, axis, root):
    mine = lax.axis_index(axis) == root
    return lax.psum(jnp.where(mine, value, jnp.zeros_like(value)), axis)


def valid_conv(padded, kernel):
    height = padded.shape[1] - 2
    width = padded.shape[2] - 2
    chans = padded.shape[0]
    windows = [
        padded[:, tap // 3 : tap // 3 + height, tap % 3 : tap % 3 + width] for tap in range(9)
    ]
    stacked = jnp.concatenate(windows, axis=0)
    flat_kernel = kernel.transpose(1, 0, 2).reshape(kernel.shape[1], 9 * chans)
    return jnp.einsum("ok,khw->ohw", flat_kernel, stacked, preferred_element_type=jnp.float32)


def with_rims(field):
    return with_halo(field, (("row", 1), ("col", 2)), 1)


def body(features, patch_index, confidence, bank, page_owner, texture_weight, conv_weight):
    tile_h = features.shape[1]
    tile_w = features.shape[2]
    flat_index = patch_index.reshape(-1)
    state = features
    for step in range(STEPS):
        owner = page_owner[step]
        local_proj = jnp.dot(texture_weight, bank[0], preferred_element_type=jnp.float32).astype(
            jnp.bfloat16
        )
        projected = broadcast(local_proj, ("row", "col"), owner)
        texture = jnp.take(projected, flat_index, axis=1).reshape(
            projected.shape[0], tile_h, tile_w
        )
        state = (state.astype(jnp.float32) + confidence[None] * texture.astype(jnp.float32)).astype(
            jnp.bfloat16
        )
        for block in range(LAYERS // 2):
            padded = with_rims(state)
            inner = jnp.maximum(valid_conv(padded, conv_weight[2 * block]), 0.0).astype(
                jnp.bfloat16
            )
            inner = with_rims(inner)
            state = (
                state.astype(jnp.float32) + valid_conv(inner, conv_weight[2 * block + 1])
            ).astype(jnp.bfloat16)
    return state


def solution(mesh):
    return jax.shard_map(
        body,
        mesh=mesh,
        in_specs=(
            P(None, "row", "col"),
            P("row", "col"),
            P("row", "col"),
            P(("row", "col"), None, None),
            P(),
            P(),
            P(),
        ),
        out_specs=P(None, "row", "col"),
        check_vma=False,
    )
```

profile of v0, /device:TPU:25, one launch (start us, length us, event | category | flops | bytes accessed | tf_op | source)
XLA Modules:
  0.0 513.0 jit_solution(1126086552741969910)
XLA Ops:
  11.6 127.7 %all-reduce.3.cloned.1.call-done = (bf16[64,2048]{1,0:T(8,128)(2,1)}, bf16[64,2048]{1,0:T(8,128)(2,1)}) async-done(((bf16[64,2048]{1,0:T(8,128)(2,1)}, bf16[64,2048]{1,0:T(8,128)(2,1)}), (bf16[64,2048]{1,0:T(8,128)(2,1)}, bf16[64,2048]{1,0:T(8,128)(2,1)})) %all-reduce.3.cloned.1.call-update) | async-done | bytes 524304 | tf_op jit(solution)/shard_map/psum | solution.py:25
  140.5 12.1 %gather_fusion = bf16[4096,64]{1,0:T(8,128)(2,1)S(1)} fusion(bf16[64,2048]{0,1:T(8,128)(2,1)S(1)} %copy.149, s32[4096]{0:T(1024)S(1)} %fusion.74), kind=kCustom, calls=%fused_computation.clone | custom fusion | bytes 1064960 | tf_op jit(solution)/shard_map/jit(_take)/gather | solution.py:55
  153.3 12.1 %gather_fusion.1 = bf16[4096,64]{1,0:T(8,128)(2,1)S(1)} fusion(bf16[64,2048]{0,1:T(8,128)(2,1)S(1)} %copy.200, s32[4096]{0:T(1024)S(1)} %fusion.74), kind=kCustom, calls=%fused_computation.1.clone | custom fusion | bytes 1064960 | tf_op jit(solution)/shard_map/jit(_take)/gather | solution.py:55
  166.8 5.3 %collective-permute-start = (bf16[64,1,128]{2,0,1:T(8,128)(2,1)S(1)}, bf16[64,1,128]{2,0,1:T(8,128)(2,1)S(1)}, u32[]{:S(2)}, u32[]{:S(2)}) collective-permute-start(bf16[64,1,128]{2,0,1:T(8,128)(2,1)S(1)} %get-tuple-element.110), channel_id=1, source_target_pairs={{0,8},{8,16},{16,24},{1,9},{9,17},{17,25},{2,10},{10,18},{18,26},{... | collective-permute-start | bytes 49160 | tf_op jit(solution)/shard_map/ppermute | solution.py:15
  180.4 3.9 collective-permute-start.3
  199.2 3.7 collective-permute-start.7
  212.4 3.4 collective-permute-start.8
  223.8 3.3 collective-permute-start.10
  254.1 3.4 collective-permute-start.16
  265.8 3.4 collective-permute-start.18
  276.6 3.4 collective-permute-start.20
  285.7 3.2 collective-permute-start.23
  298.5 3.4 collective-permute-start.24
  310.1 3.2 collective-permute-start.26
  319.2 3.8 collective-permute-start.28
  330.9 3.3 collective-permute-start.30
  360.6 3.4 collective-permute-start.36
  371.9 3.5 collective-permute-start.38
  401.4 3.4 collective-permute-start.44
  412.8 3.3 collective-permute-start.46
  433.0 3.3 collective-permute-start.50
  453.3 3.3 collective-permute-start.54
  473.5 3.6 collective-permute-start.58
  495.4 3.3 collective-permute-start.62
  (463 shorter events, 269.1 us)
Async XLA Ops:
  6.5 132.7 %all-reduce.3.cloned.1.call-start = ((), (), s32[]{:S(2)}) async-start(), calls=%async_computation | async-start | bytes 1048576 | tf_op jit(solution)/shard_map/psum | solution.py:25
  166.8 7.2 %collective-permute-start = (bf16[64,1,128]{2,0,1:T(8,128)(2,1)S(1)}, bf16[64,1,128]{2,0,1:T(8,128)(2,1)S(1)}, u32[]{:S(2)}, u32[]{:S(2)}) collective-permute-start(bf16[64,1,128]{2,0,1:T(8,128)(2,1)S(1)} %get-tuple-element.110), channel_id=1, source_target_pairs={{0,8},{8,16},{16,24},{1,9},{9,17},{17,25},{2,10},{10,18},{18,26},{... | collective-permute-start | bytes 49160 | tf_op jit(solution)/shard_map/ppermute | solution.py:15
  178.1 9.0 %collective-permute-start.2 = (bf16[64,34,1]{0,1,2:T(8,128)(2,1)S(1)}, bf16[64,34,1]{0,1,2:T(8,128)(2,1)S(1)}, u32[]{:S(2)}, u32[]{:S(2)}) collective-permute-start(bf16[64,34,1]{0,1,2:T(8,128)(2,1)S(1)} %copy.152), channel_id=1, source_target_pairs={{0,1},{1,2},{2,3},{3,4},{4,5},{5,6},{6,7},{8,9},{9,10},{10,11},{11... | collective-permute-start | bytes 13064 | tf_op jit(solution)/shard_map/ppermute | solution.py:15
  180.4 6.4 %collective-permute-start.3 = (bf16[64,34,1]{0,1,2:T(8,128)(2,1)S(1)}, bf16[64,34,1]{0,1,2:T(8,128)(2,1)S(1)}, u32[]{:S(2)}, u32[]{:S(2)}) collective-permute-start(bf16[64,34,1]{0,1,2:T(8,128)(2,1)S(1)} %copy.154), channel_id=1, source_target_pairs={{1,0},{2,1},{3,2},{4,3},{5,4},{6,5},{7,6},{9,8},{10,9},{11,10},{12... | collective-permute-start | bytes 13064 | tf_op jit(solution)/shard_map/ppermute | solution.py:18
  199.2 7.0 %collective-permute-start.7 = (bf16[64,34,1]{0,1,2:T(8,128)(2,1)S(1)}, bf16[64,34,1]{0,1,2:T(8,128)(2,1)S(1)}, u32[]{:S(2)}, u32[]{:S(2)}) collective-permute-start(bf16[64,34,1]{0,1,2:T(8,128)(2,1)S(1)} %copy.160), channel_id=1, source_target_pairs={{1,0},{2,1},{3,2},{4,3},{5,4},{6,5},{7,6},{9,8},{10,9},{11,10},{12... | collective-permute-start | bytes 13064 | tf_op jit(solution)/shard_map/ppermute | solution.py:18
  212.4 5.6 %collective-permute-start.8 = (bf16[64,1,128]{2,0,1:T(8,128)(2,1)S(1)}, bf16[64,1,128]{2,0,1:T(8,128)(2,1)S(1)}, u32[]{:S(2)}, u32[]{:S(2)}) collective-permute-start(bf16[64,1,128]{2,0,1:T(8,128)(2,1)S(1)} %get-tuple-element.106), channel_id=1, source_target_pairs={{0,8},{8,16},{16,24},{1,9},{9,17},{17,25},{2,10},{10,18},{18,26},{... | collective-permute-start | bytes 49160 | tf_op jit(solution)/shard_map/ppermute | solution.py:15
  221.6 6.4 %collective-permute-start.11 = (bf16[64,34,1]{0,1,2:T(8,128)(2,1)S(1)}, bf16[64,34,1]{0,1,2:T(8,128)(2,1)S(1)}, u32[]{:S(2)}, u32[]{:S(2)}) collective-permute-start(bf16[64,34,1]{0,1,2:T(8,128)(2,1)S(1)} %copy.166), channel_id=1, source_target_pairs={{1,0},{2,1},{3,2},{4,3},{5,4},{6,5},{7,6},{9,8},{10,9},{11,10},{12... | collective-permute-start | bytes 13064 | tf_op jit(solution)/shard_map/ppermute | solution.py:18
  241.8 7.3 %collective-permute-start.15 = (bf16[64,34,1]{0,1,2:T(8,128)(2,1)S(1)}, bf16[64,34,1]{0,1,2:T(8,128)(2,1)S(1)}, u32[]{:S(2)}, u32[]{:S(2)}) collective-permute-start(bf16[64,34,1]{0,1,2:T(8,128)(2,1)S(1)} %copy.172), channel_id=1, source_target_pairs={{1,0},{2,1},{3,2},{4,3},{5,4},{6,5},{7,6},{9,8},{10,9},{11,10},{12... | collective-permute-start | bytes 13064 | tf_op jit(solution)/shard_map/ppermute | solution.py:18
  254.1 5.4 %collective-permute-start.16 = (bf16[64,1,128]{2,0,1:T(8,128)(2,1)S(1)}, bf16[64,1,128]{2,0,1:T(8,128)(2,1)S(1)}, u32[]{:S(2)}, u32[]{:S(2)}) collective-permute-start(bf16[64,1,128]{2,0,1:T(8,128)(2,1)S(1)} %get-tuple-element.102), channel_id=1, source_target_pairs={{0,8},{8,16},{16,24},{1,9},{9,17},{17,25},{2,10},{10,18},{18,26},{... | collective-permute-start | bytes 49160 | tf_op jit(solution)/shard_map/ppermute | solution.py:15
  263.4 6.6 %collective-permute-start.19 = (bf16[64,34,1]{0,1,2:T(8,128)(2,1)S(1)}, bf16[64,34,1]{0,1,2:T(8,128)(2,1)S(1)}, u32[]{:S(2)}, u32[]{:S(2)}) collective-permute-start(bf16[64,34,1]{0,1,2:T(8,128)(2,1)S(1)} %copy.178), channel_id=1, source_target_pairs={{1,0},{2,1},{3,2},{4,3},{5,4},{6,5},{7,6},{9,8},{10,9},{11,10},{12... | collective-permute-start | bytes 13064 | tf_op jit(solution)/shard_map/ppermute | solution.py:18
  285.7 7.3 %collective-permute-start.23 = (bf16[64,34,1]{0,1,2:T(8,128)(2,1)S(1)}, bf16[64,34,1]{0,1,2:T(8,128)(2,1)S(1)}, u32[]{:S(2)}, u32[]{:S(2)}) collective-permute-start(bf16[64,34,1]{0,1,2:T(8,128)(2,1)S(1)} %copy.184), channel_id=1, source_target_pairs={{1,0},{2,1},{3,2},{4,3},{5,4},{6,5},{7,6},{9,8},{10,9},{11,10},{12... | collective-permute-start | bytes 13064 | tf_op jit(solution)/shard_map/ppermute | solution.py:18
  298.5 5.4 %collective-permute-start.24 = (bf16[64,1,128]{2,0,1:T(8,128)(2,1)S(1)}, bf16[64,1,128]{2,0,1:T(8,128)(2,1)S(1)}, u32[]{:S(2)}, u32[]{:S(2)}) collective-permute-start(bf16[64,1,128]{2,0,1:T(8,128)(2,1)S(1)} %get-tuple-element.98), channel_id=1, source_target_pairs={{0,8},{8,16},{16,24},{1,9},{9,17},{17,25},{2,10},{10,18},{18,26},{... | collective-permute-start | bytes 49160 | tf_op jit(solution)/shard_map/ppermute | solution.py:15
  307.7 5.8 %collective-permute-start.27 = (bf16[64,34,1]{0,1,2:T(8,128)(2,1)S(1)}, bf16[64,34,1]{0,1,2:T(8,128)(2,1)S(1)}, u32[]{:S(2)}, u32[]{:S(2)}) collective-permute-start(bf16[64,34,1]{0,1,2:T(8,128)(2,1)S(1)} %copy.190), channel_id=1, source_target_pairs={{1,0},{2,1},{3,2},{4,3},{5,4},{6,5},{7,6},{9,8},{10,9},{11,10},{12... | collective-permute-start | bytes 13064 | tf_op jit(solution)/shard_map/ppermute | solution.py:18
  319.2 5.7 %collective-permute-start.28 = (bf16[64,1,128]{2,0,1:T(8,128)(2,1)S(1)}, bf16[64,1,128]{2,0,1:T(8,128)(2,1)S(1)}, u32[]{:S(2)}, u32[]{:S(2)}) collective-permute-start(bf16[64,1,128]{2,0,1:T(8,128)(2,1)S(1)} %get-tuple-element.96), channel_id=1, source_target_pairs={{0,8},{8,16},{16,24},{1,9},{9,17},{17,25},{2,10},{10,18},{18,26},{... | collective-permute-start | bytes 49160 | tf_op jit(solution)/shard_map/ppermute | solution.py:15
  328.7 7.3 %collective-permute-start.31 = (bf16[64,34,1]{0,1,2:T(8,128)(2,1)S(1)}, bf16[64,34,1]{0,1,2:T(8,128)(2,1)S(1)}, u32[]{:S(2)}, u32[]{:S(2)}) collective-permute-start(bf16[64,34,1]{0,1,2:T(8,128)(2,1)S(1)} %copy.196), channel_id=1, source_target_pairs={{1,0},{2,1},{3,2},{4,3},{5,4},{6,5},{7,6},{9,8},{10,9},{11,10},{12... | collective-permute-start | bytes 13064 | tf_op jit(solution)/shard_map/ppermute | solution.py:18
  330.9 5.4 %collective-permute-start.30 = (bf16[64,34,1]{0,1,2:T(8,128)(2,1)S(1)}, bf16[64,34,1]{0,1,2:T(8,128)(2,1)S(1)}, u32[]{:S(2)}, u32[]{:S(2)}) collective-permute-start(bf16[64,34,1]{0,1,2:T(8,128)(2,1)S(1)} %copy.194), channel_id=1, source_target_pairs={{0,1},{1,2},{2,3},{3,4},{4,5},{5,6},{6,7},{8,9},{9,10},{10,11},{11... | collective-permute-start | bytes 13064 | tf_op jit(solution)/shard_map/ppermute | solution.py:15
  349.0 5.6 %collective-permute-start.35 = (bf16[64,34,1]{0,1,2:T(8,128)(2,1)S(1)}, bf16[64,34,1]{0,1,2:T(8,128)(2,1)S(1)}, u32[]{:S(2)}, u32[]{:S(2)}) collective-permute-start(bf16[64,34,1]{0,1,2:T(8,128)(2,1)S(1)} %copy.205), channel_id=1, source_target_pairs={{1,0},{2,1},{3,2},{4,3},{5,4},{6,5},{7,6},{9,8},{10,9},{11,10},{12... | collective-permute-start | bytes 13064 | tf_op jit(solution)/shard_map/ppermute | solution.py:18
  369.7 5.8 %collective-permute-start.39 = (bf16[64,34,1]{0,1,2:T(8,128)(2,1)S(1)}, bf16[64,34,1]{0,1,2:T(8,128)(2,1)S(1)}, u32[]{:S(2)}, u32[]{:S(2)}) collective-permute-start(bf16[64,34,1]{0,1,2:T(8,128)(2,1)S(1)} %copy.210), channel_id=1, source_target_pairs={{1,0},{2,1},{3,2},{4,3},{5,4},{6,5},{7,6},{9,8},{10,9},{11,10},{12... | collective-permute-start | bytes 13064 | tf_op jit(solution)/shard_map/ppermute | solution.py:18
  389.9 5.6 %collective-permute-start.43 = (bf16[64,34,1]{0,1,2:T(8,128)(2,1)S(1)}, bf16[64,34,1]{0,1,2:T(8,128)(2,1)S(1)}, u32[]{:S(2)}, u32[]{:S(2)}) collective-permute-start(bf16[64,34,1]{0,1,2:T(8,128)(2,1)S(1)} %copy.215), channel_id=1, source_target_pairs={{1,0},{2,1},{3,2},{4,3},{5,4},{6,5},{7,6},{9,8},{10,9},{11,10},{12... | collective-permute-start | bytes 13064 | tf_op jit(solution)/shard_map/ppermute | solution.py:18
  410.5 5.6 %collective-permute-start.47 = (bf16[64,34,1]{0,1,2:T(8,128)(2,1)S(1)}, bf16[64,34,1]{0,1,2:T(8,128)(2,1)S(1)}, u32[]{:S(2)}, u32[]{:S(2)}) collective-permute-start(bf16[64,34,1]{0,1,2:T(8,128)(2,1)S(1)} %copy.220), channel_id=1, source_target_pairs={{1,0},{2,1},{3,2},{4,3},{5,4},{6,5},{7,6},{9,8},{10,9},{11,10},{12... | collective-permute-start | bytes 13064 | tf_op jit(solution)/shard_map/ppermute | solution.py:18
  430.8 5.6 %collective-permute-start.51 = (bf16[64,34,1]{0,1,2:T(8,128)(2,1)S(1)}, bf16[64,34,1]{0,1,2:T(8,128)(2,1)S(1)}, u32[]{:S(2)}, u32[]{:S(2)}) collective-permute-start(bf16[64,34,1]{0,1,2:T(8,128)(2,1)S(1)} %copy.225), channel_id=1, source_target_pairs={{1,0},{2,1},{3,2},{4,3},{5,4},{6,5},{7,6},{9,8},{10,9},{11,10},{12... | collective-permute-start | bytes 13064 | tf_op jit(solution)/shard_map/ppermute | solution.py:18
  451.0 5.6 %collective-permute-start.55 = (bf16[64,34,1]{0,1,2:T(8,128)(2,1)S(1)}, bf16[64,34,1]{0,1,2:T(8,128)(2,1)S(1)}, u32[]{:S(2)}, u32[]{:S(2)}) collective-permute-start(bf16[64,34,1]{0,1,2:T(8,128)(2,1)S(1)} %copy.230), channel_id=1, source_target_pairs={{1,0},{2,1},{3,2},{4,3},{5,4},{6,5},{7,6},{9,8},{10,9},{11,10},{12... | collective-permute-start | bytes 13064 | tf_op jit(solution)/shard_map/ppermute | solution.py:18
  471.3 5.9 %collective-permute-start.59 = (bf16[64,34,1]{0,1,2:T(8,128)(2,1)S(1)}, bf16[64,34,1]{0,1,2:T(8,128)(2,1)S(1)}, u32[]{:S(2)}, u32[]{:S(2)}) collective-permute-start(bf16[64,34,1]{0,1,2:T(8,128)(2,1)S(1)} %copy.235), channel_id=1, source_target_pairs={{1,0},{2,1},{3,2},{4,3},{5,4},{6,5},{7,6},{9,8},{10,9},{11,10},{12... | collective-permute-start | bytes 13064 | tf_op jit(solution)/shard_map/ppermute | solution.py:18
  493.2 5.6 %collective-permute-start.63 = (bf16[64,34,1]{0,1,2:T(8,128)(2,1)S(1)}, bf16[64,34,1]{0,1,2:T(8,128)(2,1)S(1)}, u32[]{:S(2)}, u32[]{:S(2)}) collective-permute-start(bf16[64,34,1]{0,1,2:T(8,128)(2,1)S(1)} %copy.240), channel_id=1, source_target_pairs={{1,0},{2,1},{3,2},{4,3},{5,4},{6,5},{7,6},{9,8},{10,9},{11,10},{12... | collective-permute-start | bytes 13064 | tf_op jit(solution)/shard_map/ppermute | solution.py:18
  (64 other events, 289.4 us)
Sparse Core Ops, SparseCore 0:
  12.8 126.3 all-reduce.2
where the time goes:
time: 523 us; the launch traced here: 513 us
  waiting for transfers between devices  197 us (38%)
  starting transfers between devices  171 us (33%)
  local copies, waits for them, and re-layouts  89.8 us (17%)
  matrix products  19 us (4%)
  other arithmetic  18.7 us (4%)
  between operations  18.1 us (3%)
    psum x1, waiting for transfers between devices, broadcast(): return lax.psum(jnp.where(mine, value, jnp.zeros_like(value)), axis)  128 us
    ppermute x32, starting transfers between devices, with_halo(): lax.ppermute(lax.slice_in_dim(block, block.shape[dim] - width, None, axis...  102 us
    ppermute x32, starting transfers between devices, with_halo(): lax.ppermute(lax.slice_in_dim(block, 0, width, axis=dim), axis, backward)  68.7 us
    ppermute x32, waiting for transfers between devices, with_halo(): lax.ppermute(lax.slice_in_dim(block, 0, width, axis=dim), axis, backward)  49.6 us
    gather x4, local copies, waits for them, and re-layouts, body(): jnp.take(projected, flat_index, axis=1)  24.9 us
    ppermute x32, waiting for transfers between devices, with_halo(): lax.ppermute(lax.slice_in_dim(block, block.shape[dim] - width, None, axis...  19.4 us
    unnamed x142, local copies, waits for them, and re-layouts  18 us
    dot_general x16, matrix products, valid_conv(): jnp.einsum('ok,khw->ohw', flat_kernel, stacked, preferred_element_type=jn...  16.8 us
  transfers between devices with their start and end apart: 65, of which 31 were waited for; matrix products, arithmetic and copies ran while one was open for 4% of the time, Pallas kernels for 0%

commit v1 on v0

v1 whole, which is shorter than its diff:
```python
import functools

import jax
import jax.numpy as jnp
from jax import lax
from jax.experimental import pallas as pl
from jax.experimental.pallas import tpu as pltpu
from jax.sharding import PartitionSpec as P

LAYERS = 8
STEPS = 2
HALO = LAYERS * STEPS
LOW = 256
SLICE = 16
AROUND = [(-1, -1), (-1, 0), (-1, 1), (0, -1), (0, 1), (1, -1), (1, 0), (1, 1)]
MESH = pl.DeviceIdType.MESH
VMEM = pl.BlockSpec(memory_space=pltpu.VMEM)
SMEM = pl.BlockSpec(memory_space=pltpu.SMEM)


def project_kernel(weight_ref, bank_ref, out_ref):
    out_ref[...] = jnp.dot(
        weight_ref[...], bank_ref[0], preferred_element_type=jnp.float32
    ).astype(jnp.bfloat16)


def project(texture_weight, bank):
    chans, depth = texture_weight.shape
    high = bank.shape[2] // LOW
    return pl.pallas_call(
        project_kernel,
        grid=(high,),
        in_specs=[
            pl.BlockSpec((chans, depth), lambda h: (0, 0)),
            pl.BlockSpec((1, depth, LOW), lambda h: (0, 0, h)),
        ],
        out_specs=pl.BlockSpec((chans, LOW), lambda h: (h, 0)),
        out_shape=jax.ShapeDtypeStruct((high * chans, LOW), jnp.bfloat16),
    )(texture_weight, bank)


def exchange_kernel(
    rows, cols, hubs,
    owner_ref, proj_ref, state_ref, left_ref, right_ref, aux_ref,
    pages_ref, above_ref, below_ref, onleft_ref, onright_ref, around_ref,
    slots, spread_send, spread_recv, gather_send, gather_recv,
    halo_send, halo_recv, aux_send, aux_recv,
):
    my_row, my_col = lax.axis_index("row"), lax.axis_index("col")
    count = rows * cols
    me = my_row * cols + my_col

    def place(index):
        return (index // cols, lax.rem(index, cols))

    def spread(source_slice, slot, target):
        return pltpu.make_async_remote_copy(
            src_ref=proj_ref.at[pl.ds(pl.multiple_of(source_slice * SLICE, SLICE), SLICE), :],
            dst_ref=slots.at[slot],
            send_sem=spread_send.at[target],
            recv_sem=spread_recv.at[slot],
            device_id=place(target),
            device_id_type=MESH,
        )

    def gather(part, target):
        part_ref = pages_ref.at[:, pl.ds(pl.multiple_of(part * SLICE, SLICE), SLICE), :]
        return pltpu.make_async_remote_copy(
            src_ref=part_ref,
            dst_ref=part_ref,
            send_sem=gather_send.at[target],
            recv_sem=gather_recv.at[part],
            device_id=place(target),
            device_id_type=MESH,
        )

    def each_other(limit, action):
        def step(k, carry):
            other = lax.rem(me + k, count)
            if limit == count:
                action(other)
            else:
                pl.when(other < limit)(lambda: action(other))
            return carry

        lax.fori_loop(1, count, step, 0)

    def if_hub(action):
        if hubs == count:
            action()
        else:
            pl.when(me < hubs)(action)

    half = HALO
    quarter = left_ref.shape[0] // 2

    def halo(k):
        dr, dc = AROUND[k]
        if dc == 0:
            source = state_ref.at[pl.ds(0 if dr < 0 else half, half)]
            dest = below_ref if dr < 0 else above_ref
        else:
            edge = left_ref if dc < 0 else right_ref
            land = onright_ref if dc < 0 else onleft_ref
            if dr == 0:
                source, dest = edge, land.at[pl.ds(quarter, 2 * quarter)]
            elif dr < 0:
                source, dest = edge.at[pl.ds(0, quarter)], land.at[pl.ds(3 * quarter, quarter)]
            else:
                source, dest = edge.at[pl.ds(quarter, quarter)], land.at[pl.ds(0, quarter)]
        target = (lax.rem(my_row + dr + rows, rows), lax.rem(my_col + dc + cols, cols))
        first = pltpu.make_async_remote_copy(
            src_ref=source, dst_ref=dest, send_sem=halo_send.at[k], recv_sem=halo_recv.at[k],
            device_id=target, device_id_type=MESH,
        )
        second = pltpu.make_async_remote_copy(
            src_ref=aux_ref, dst_ref=around_ref.at[7 - k], send_sem=aux_send.at[k],
            recv_sem=aux_recv.at[k], device_id=target, device_id_type=MESH,
        )
        return first, second

    each_other(hubs, lambda other: spread(other, me, other).start())
    halos = [copy for k in range(8) for copy in halo(k)]
    for copy in halos:
        copy.start()

    def pick():
        slots[me] = proj_ref[pl.ds(pl.multiple_of(me * SLICE, SLICE), SLICE), :]
        each_other(count, lambda other: spread(0, other, other).wait_recv())
        for step in range(STEPS):
            pages_ref[step, pl.ds(pl.multiple_of(me * SLICE, SLICE), SLICE), :] = slots[
                owner_ref[step]
            ]
        each_other(count, lambda other: gather(me, other).start())

    if_hub(pick)
    each_other(hubs, lambda other: spread(other, me, other).wait_send())
    each_other(hubs, lambda other: gather(other, other).wait_recv())
    if_hub(lambda: each_other(count, lambda other: gather(me, other).wait_send()))
    for copy in halos:
        copy.wait()


def exchange(rows, cols, page_owner, proj, state, left, right, aux):
    count = rows * cols
    hubs = min(count, proj.shape[0] // SLICE)
    tile_h, chans, tile_w = state.shape
    edge = (2 * left.shape[0],) + left.shape[1:]
    bf16 = jnp.bfloat16
    dma = pltpu.SemaphoreType.DMA
    return pl.pallas_call(
        functools.partial(exchange_kernel, rows, cols, hubs),
        in_specs=[SMEM] + [VMEM] * 5,
        out_specs=[VMEM] * 6,
        out_shape=[
            jax.ShapeDtypeStruct((STEPS,) + proj.shape, bf16),
            jax.ShapeDtypeStruct((HALO, chans, tile_w), bf16),
            jax.ShapeDtypeStruct((HALO, chans, tile_w), bf16),
            jax.ShapeDtypeStruct(edge, bf16),
            jax.ShapeDtypeStruct(edge, bf16),
            jax.ShapeDtypeStruct((8,) + aux.shape, jnp.float32),
        ],
        scratch_shapes=[
            pltpu.VMEM((count, SLICE, LOW), bf16),
            dma((count,)), dma((count,)), dma((count,)), dma((count,)),
            dma((8,)), dma((8,)), dma((8,)), dma((8,)),
        ],
        compiler_params=pltpu.CompilerParams(
            has_side_effects=True, vmem_limit_bytes=32 * 1024 * 1024
        ),
    )(page_owner, proj, state, left, right, aux)


def trunk_kernel(
    rows, cols,
    pages_ref, state_ref, above_ref, below_ref, onleft_ref, onright_ref, aux_ref, around_ref,
    weight_ref, out_ref,
    field, inner, second, patch, trust,
):
    my_row, my_col = lax.axis_index("row"), lax.axis_index("col")
    tile_h, chans, tile_w = state_ref.shape
    full_h, lanes = tile_h + 2 * HALO, 2 * tile_w
    per = tile_w // HALO
    half = tile_w // 2

    lane = lax.broadcasted_iota(jnp.int32, (1, lanes), 1)
    column = jnp.where(lane < lanes - half, lane, lane - lanes)
    in_view = (column >= -HALO) & (column < tile_w + HALO)
    column = column + my_col * tile_w
    in_cols = in_view & (column >= 0) & (column < cols * tile_w)
    top = my_row * tile_h - HALO

    def keep(i):
        row = top + i
        inside = (row >= 0) & (row < rows * tile_h)
        return jnp.where(in_cols, inside.astype(jnp.int32), 0) > 0

    narrow = lax.broadcasted_iota(jnp.int32, (1, tile_w), 1) < half
    for which, target in ((0, patch), (1, trust)):
        for start, size, begin, trio in (
            (0, HALO, tile_h - HALO, (0, 1, 2)),
            (HALO, tile_h, 0, (3, None, 4)),
            (HALO + tile_h, HALO, 0, (5, 6, 7)),
        ):
            low, mid, high = [
                (aux_ref if k is None else around_ref.at[k])[which, pl.ds(begin, size), :]
                for k in trio
            ]
            target[pl.ds(start, size), :tile_w] = mid
            target[pl.ds(start, size), tile_w:] = jnp.where(narrow, high, low)

    row_of = lax.broadcasted_iota(jnp.int32, (LOW, lanes), 0)
    count_high = pages_ref.shape[1] // chans

    def begin_row(ref, at, group, spot, i):
        number = patch[pl.ds(i, 1), :].astype(jnp.int32)
        high = lax.shift_right_logical(number, 8)
        hot = jnp.where(row_of == (number & (LOW - 1)), 1.0, 0.0).astype(jnp.bfloat16)
        values = []
        for step in range(STEPS):
            every = jnp.dot(pages_ref[step], hot, preferred_element_type=jnp.float32)
            value = every[:chans]
            for h in range(1, count_high):
                value = jnp.where(high == h, every[h * chans : (h + 1) * chans], value)
            values.append(value)
        main = ref[at].astype(jnp.float32)
        right = pltpu.roll(onright_ref[group].astype(jnp.float32), (tile_w - spot * HALO) % tile_w, 1)
        left = pltpu.roll(onleft_ref[group].astype(jnp.float32), tile_w - HALO - spot * HALO, 1)
        start = jnp.concatenate([main, jnp.where(narrow, right, left)], axis=1)
        start = start + trust[pl.ds(i, 1), :] * values[0]
        field[i + 1] = jnp.where(keep(i), start, 0.0).astype(jnp.bfloat16)
        second[i] = values[1].astype(jnp.bfloat16)

    for ref, start, size in ((above_ref, 0, HALO), (state_ref, HALO, tile_h), (below_ref, HALO + tile_h, HALO)):
        def begin_group(g, carry, ref=ref, start=start):
            for spot in range(per):
                begin_row(ref, g * per + spot, start // per + g, spot, start + g * per + spot)
            return carry

        lax.fori_loop(0, size // per, begin_group, 0)

    unroll = 4
    for layer in range(STEPS * LAYERS):
        source, target = (field, inner) if layer % 2 == 0 else (inner, field)
        if layer == LAYERS:
            def again(i, carry):
                value = field[i + 1].astype(jnp.float32)
                value = value + trust[pl.ds(i, 1), :] * second[i].astype(jnp.float32)
                field[i + 1] = jnp.where(keep(i), value, 0.0).astype(jnp.bfloat16)
                return carry

            lax.fori_loop(layer, full_h - layer, again, 0)
        first = layer - layer % 2
        total = full_h - 2 * first

        def conv_rows(g, carry, layer=layer, first=first, source=source, target=target):
            early, late = carry
            kernel = weight_ref[layer % LAYERS]
            for u in range(unroll):
                r = first + g * unroll + u
                value = source[r + 1]
                stacked = jnp.concatenate(
                    [pltpu.roll(value, 1, 1), value, pltpu.roll(value, lanes - 1, 1)], axis=0
                )
                product = jnp.dot(kernel, stacked, preferred_element_type=jnp.float32)
                done = late + product[2 * chans :]
                late = early + product[chans : 2 * chans]
                early = product[:chans]
                if layer % 2 == 0:
                    done = jnp.maximum(done, 0.0)
                else:
                    done = field[r].astype(jnp.float32) + done
                target[r] = jnp.where(keep(r - 1), done, 0.0).astype(jnp.bfloat16)
            return early, late

        zero = jnp.zeros((chans, lanes), jnp.float32)
        lax.fori_loop(0, total // unroll, conv_rows, (zero, zero))

    out_ref[...] = field[pl.ds(HALO + 1, tile_h), :, :tile_w]


def trunk(rows, cols, pages, state, above, below, onleft, onright, aux, around, weights):
    tile_h, chans, tile_w = state.shape
    full_h, lanes = tile_h + 2 * HALO, 2 * tile_w
    return pl.pallas_call(
        functools.partial(trunk_kernel, rows, cols),
        in_specs=[VMEM] * 9,
        out_specs=VMEM,
        out_shape=jax.ShapeDtypeStruct(state.shape, jnp.bfloat16),
        scratch_shapes=[
            pltpu.VMEM((full_h + 2, chans, lanes), jnp.bfloat16),
            pltpu.VMEM((full_h + 2, chans, lanes), jnp.bfloat16),
            pltpu.VMEM((full_h, chans, lanes), jnp.bfloat16),
            pltpu.VMEM((full_h, lanes), jnp.float32),
            pltpu.VMEM((full_h, lanes), jnp.float32),
        ],
        compiler_params=pltpu.CompilerParams(vmem_limit_bytes=48 * 1024 * 1024),
    )(pages, state, above, below, onleft, onright, aux, around, weights)


def packed(edge, tile_w):
    tile_h, chans, width = edge.shape
    per = tile_w // width
    return edge.reshape(tile_h // per, per, chans, width).transpose(0, 2, 1, 3).reshape(
        tile_h // per, chans, tile_w
    )


def body(rows, cols, features, patch_index, confidence, bank, page_owner, texture_weight, conv_weight):
    chans, tile_h, tile_w = features.shape
    proj = project(texture_weight, bank)
    state = features.transpose(1, 0, 2)
    left = packed(state[:, :, :HALO], tile_w)
    right = packed(state[:, :, tile_w - HALO :], tile_w)
    aux = jnp.stack([patch_index.astype(jnp.float32), confidence])
    weights = (
        conv_weight.reshape(LAYERS, 3, 3, chans, chans)
        .transpose(0, 1, 3, 2, 4)
        .reshape(LAYERS, 3 * chans, 3 * chans)
    )
    received = exchange(rows, cols, page_owner, proj, state, left, right, aux)
    pages, above, below, onleft, onright, around = received
    out = trunk(rows, cols, pages, state, above, below, onleft, onright, aux, around, weights)
    return out.transpose(1, 0, 2)


def solution(mesh):
    return jax.shard_map(
        functools.partial(body, mesh.shape["row"], mesh.shape["col"]),
        mesh=mesh,
        in_specs=(
            P(None, "row", "col"),
            P("row", "col"),
            P("row", "col"),
            P(("row", "col"), None, None),
            P(),
            P(),
            P(),
        ),
        out_specs=P(None, "row", "col"),
        check_vma=False,
    )
```

time: 523 us -> 134 us (0.26)
  the two profiles are of different devices: /device:TPU:25 before, /device:TPU:0 now
where the time goes in v1:
time: 134 us; the launch traced here: 133 us
  Pallas kernels  123 us (92%)
  local copies, waits for them, and re-layouts  8.77 us (7%)
  other arithmetic  1.5 us (1%)
    pallas_call x1, Pallas kernels, trunk(): pl.pallas_call(functools.partial(trunk_kernel, rows, cols), in_specs=[VME...  79.5 us
    pallas_call x1, Pallas kernels, exchange(): pl.pallas_call(functools.partial(exchange_kernel, rows, cols, hubs), in_s...  37.3 us
    pallas_call x1, Pallas kernels, project(): pl.pallas_call(project_kernel, grid=(high,), in_specs=[pl.BlockSpec((chan...  5.94 us
    reshape x1, local copies, waits for them, and re-layouts, body(): conv_weight.reshape(LAYERS, 3, 3, chans, chans).transpose(0, 1, 3, 2, 4)  3.51 us
    reshape x1, local copies, waits for them, and re-layouts, body(): weights = conv_weight.reshape(LAYERS, 3, 3, chans, chans).transpose(0, 1,...  3 us

profile of v1, /device:TPU:0, one launch (start us, length us, event | category | flops | bytes accessed | tf_op | source)
XLA Modules:
  0.0 133.1 jit_solution(14422777472779450258)
XLA Ops:
  0.0 0.0 copy-start.2
  0.0 0.8 convert_bitcast_fusion
  0.8 0.7 pad_maximum_fusion.aux_ref
  1.5 5.9 %shard_map.73.proj_ref = bf16[512,256]{1,0:T(8,128)(2,1)} custom-call(bf16[64,576]{1,0:T(8,128)(2,1)} %weight_ref.1, bf16[1,576,2048]{2,1,0:T(8,128)(2,1)} %bank_ref.1), custom_call_target="tpu_custom_call" | custom-call | tf_op jit(solution)/shard_map/pallas_call | solution.py:30
  7.4 0.0 copy-done.2
  7.4 0.2 copy.23
  7.6 0.0 copy-start
  7.7 0.0 copy-start.1
  7.7 0.2 fusion
  7.9 0.2 copy.15
  8.1 0.1 copy.17.right_ref
  8.3 0.2 copy.14
  8.5 0.1 copy.16.left_ref
  8.6 0.0 copy-done
  8.6 0.0 copy-done.1
  8.6 37.3 %shard_map.74 = (bf16[2,512,256]{2,1,0:T(8,128)(2,1)S(1)}, bf16[16,64,128]{2,1,0:T(8,128)(2,1)S(1)}, bf16[16,64,128]{2,1,0:T(8,128)(2,1)S(1)}, bf16[8,64,128]{2,...) custom-call(s32[2]{0:T(128)S(1)} %copy-done.1, bf16[512,256]{1,0:T(8,128)(2,1)S(1)} %copy-done, ...), custom_call_target="tpu_custom_call" | custom-call | tf_op jit(solution)/shard_map/pallas_call | solution.py:151
  45.9 3.5 %copy.22 = bf16[8,3,3,64,64]{4,2,3,1,0:T(4,128)(2,1)} copy(bf16[8,3,3,64,64]{4,3,2,1,0:T(8,128)(2,1)} %bitcast.26) | data formatting | bytes 1179648 | tf_op jit(solution)/shard_map/reshape | solution.py:317
  49.5 3.0 %reshape.23.weight_ref = bf16[8,192,192]{2,1,0:T(8,128)(2,1)S(1)} reshape(bf16[8,3,64,3,64]{4,3,2,1,0:T(4,128)(2,1)} %bitcast.23) | data formatting | bytes 1179648 | tf_op jit(solution)/shard_map/reshape | solution.py:319
  52.5 79.5 %shard_map.75 = bf16[32,64,128]{2,1,0:T(8,128)(2,1)S(1)} custom-call(bf16[2,512,256]{2,1,0:T(8,128)(2,1)S(1)} %get-tuple-element.11.pages_ref, bf16[32,64,128]{2,1,0:T(8,128)(2,1)S(1)} %bitcast.21, bf16[16,64,128]{2,1,0:T(8,128)(2,1)S(1)} %get-tuple-element.12.above_ref, bf16[16,64,128]{2,1,0:T(8,128)(2,1)S(1)} %get-tuple-element.13.below_ref, ...), custom_call_target="tpu_custom_call" | custom-call | tf_op jit(solution)/shard_map/pallas_call | solution.py:285
  131.9 1.1 copy.19
Async XLA Ops:
  0.0 7.4 %copy-start.2 = (bf16[64,32,128]{2,1,0:T(8,128)(2,1)S(1)}, bf16[64,32,128]{2,1,0:T(8,128)(2,1)}, u32[]{:S(2)}) copy-start(bf16[64,32,128]{2,1,0:T(8,128)(2,1)} %param.7) | copy-start | bytes 1572868
  7.6 1.0 copy-start
  7.7 0.9 copy-start.1

commit v2 on v1

--- a/solution.py
+++ b/solution.py
@@ -10,6 +10,7 @@
 LAYERS = 8
 STEPS = 2
 HALO = LAYERS * STEPS
+UNROLL = 32
 LOW = 256
 SLICE = 16
 AROUND = [(-1, -1), (-1, 0), (-1, 1), (0, -1), (0, 1), (1, -1), (1, 0), (1, 1)]
@@ -41,8 +42,8 @@
 
 def exchange_kernel(
     rows, cols, hubs,
-    owner_ref, proj_ref, state_ref, left_ref, right_ref, aux_ref,
-    pages_ref, above_ref, below_ref, onleft_ref, onright_ref, around_ref,
+    owner_ref, proj_ref, state_ref, left_ref, right_ref, aux_ref, taps_ref,
+    pages_ref, above_ref, below_ref, onleft_ref, onright_ref, around_ref, weight_ref,
     slots, spread_send, spread_recv, gather_send, gather_recv,
     halo_send, halo_recv, aux_send, aux_recv,
 ):
@@ -120,9 +121,25 @@
         return first, second
 
     each_other(hubs, lambda other: spread(other, me, other).start())
-    halos = [copy for k in range(8) for copy in halo(k)]
-    for copy in halos:
-        copy.start()
+    def in_window(row, col):
+        return (row >= 0) & (row < rows) & (col >= 0) & (col < cols)
+
+    for k, (dr, dc) in enumerate(AROUND):
+        @pl.when(in_window(my_row + dr, my_col + dc))
+        def _(k=k):
+            for copy in halo(k):
+                copy.start()
+
+    chans = taps_ref.shape[2]
+
+    def arrange(layer, carry):
+        for dy in range(3):
+            weight_ref[layer, dy * chans : (dy + 1) * chans, :] = jnp.concatenate(
+                [taps_ref[layer, 3 * dy + dx] for dx in range(3)], axis=1
+            )
+        return carry
+
+    lax.fori_loop(0, LAYERS, arrange, 0)
 
     def pick():
         slots[me] = proj_ref[pl.ds(pl.multiple_of(me * SLICE, SLICE), SLICE), :]
@@ -137,11 +154,19 @@
     each_other(hubs, lambda other: spread(other, me, other).wait_send())
     each_other(hubs, lambda other: gather(other, other).wait_recv())
     if_hub(lambda: each_other(count, lambda other: gather(me, other).wait_send()))
-    for copy in halos:
-        copy.wait()
-
-
-def exchange(rows, cols, page_owner, proj, state, left, right, aux):
+    for k, (dr, dc) in enumerate(AROUND):
+        @pl.when(in_window(my_row + dr, my_col + dc))
+        def _(k=k):
+            for copy in halo(k):
+                copy.wait_send()
+
+        @pl.when(in_window(my_row - dr, my_col - dc))
+        def _(k=k):
+            for copy in halo(k):
+                copy.wait_recv()
+
+
+def exchange(rows, cols, page_owner, proj, state, left, right, aux, taps):
     count = rows * cols
     hubs = min(count, proj.shape[0] // SLICE)
     tile_h, chans, tile_w = state.shape
@@ -150,8 +175,8 @@
     dma = pltpu.SemaphoreType.DMA
     return pl.pallas_call(
         functools.partial(exchange_kernel, rows, cols, hubs),
-        in_specs=[SMEM] + [VMEM] * 5,
-        out_specs=[VMEM] * 6,
+        in_specs=[SMEM] + [VMEM] * 6,
+        out_specs=[VMEM] * 7,
         out_shape=[
             jax.ShapeDtypeStruct((STEPS,) + proj.shape, bf16),
             jax.ShapeDtypeStruct((HALO, chans, tile_w), bf16),
@@ -159,6 +184,7 @@
             jax.ShapeDtypeStruct(edge, bf16),
             jax.ShapeDtypeStruct(edge, bf16),
             jax.ShapeDtypeStruct((8,) + aux.shape, jnp.float32),
+            jax.ShapeDtypeStruct((LAYERS, 3 * chans, 3 * chans), bf16),
         ],
         scratch_shapes=[
             pltpu.VMEM((count, SLICE, LOW), bf16),
@@ -168,7 +194,7 @@
         compiler_params=pltpu.CompilerParams(
             has_side_effects=True, vmem_limit_bytes=32 * 1024 * 1024
         ),
-    )(page_owner, proj, state, left, right, aux)
+    )(page_owner, proj, state, left, right, aux, taps)
 
 
 def trunk_kernel(
@@ -239,7 +265,6 @@
 
         lax.fori_loop(0, size // per, begin_group, 0)
 
-    unroll = 4
     for layer in range(STEPS * LAYERS):
         source, target = (field, inner) if layer % 2 == 0 else (inner, field)
         if layer == LAYERS:
@@ -252,8 +277,9 @@
             lax.fori_loop(layer, full_h - layer, again, 0)
         first = layer - layer % 2
         total = full_h - 2 * first
-
-        def conv_rows(g, carry, layer=layer, first=first, source=source, target=target):
+        unroll = max(d for d in range(1, UNROLL + 1) if total % d == 0)
+
+        def conv_rows(g, carry, layer=layer, unroll=unroll, first=first, source=source, target=target):
             early, late = carry
             kernel = weight_ref[layer % LAYERS]
             for u in range(unroll):
@@ -313,13 +339,8 @@
     left = packed(state[:, :, :HALO], tile_w)
     right = packed(state[:, :, tile_w - HALO :], tile_w)
     aux = jnp.stack([patch_index.astype(jnp.float32), confidence])
-    weights = (
-        conv_weight.reshape(LAYERS, 3, 3, chans, chans)
-        .transpose(0, 1, 3, 2, 4)
-        .reshape(LAYERS, 3 * chans, 3 * chans)
-    )
-    received = exchange(rows, cols, page_owner, proj, state, left, right, aux)
-    pages, above, below, onleft, onright, around = received
+    received = exchange(rows, cols, page_owner, proj, state, left, right, aux, conv_weight)
+    pages, above, below, onleft, onright, around, weights = received
     out = trunk(rows, cols, pages, state, above, below, onleft, onright, aux, around, weights)
     return out.transpose(1, 0, 2)
 

time: 134 us -> 84.9 us (0.63)
  Pallas kernels: 123 us -> 80.6 us
  local copies, waits for them, and re-layouts: 8.77 us -> 2.41 us
    pallas_call x1, Pallas kernels: 79.5 us -> 40 us  [trunk(): pl.pallas_call(functools.partial(trunk_kernel, rows, cols), in_specs=[VME...]
    reshape x2 -> x0, local copies, waits for them, and re-layouts: 6.51 us -> none  [the longest x1 3.51 us: body(): conv_weight.reshape(LAYERS, 3, 3, chans, chans).transpose(0, 1, 3, 2, 4)]
    pallas_call x1, Pallas kernels: 37.3 us -> 34.7 us  [exchange(): pl.pallas_call(functools.partial(exchange_kernel, rows, cols, hubs), in_s...]
where the time goes in v2:
time: 84.9 us; the launch traced here: 84.6 us
  Pallas kernels  80.6 us (95%)
  local copies, waits for them, and re-layouts  2.41 us (3%)
  other arithmetic  1.5 us (2%)
    pallas_call x1, Pallas kernels, trunk(): pl.pallas_call(functools.partial(trunk_kernel, rows, cols), in_specs=[VME...  40 us
    pallas_call x1, Pallas kernels, exchange(): pl.pallas_call(functools.partial(exchange_kernel, rows, cols, hubs), in_s...  34.7 us
    pallas_call x1, Pallas kernels, project(): pl.pallas_call(project_kernel, grid=(high,), in_specs=[pl.BlockSpec((chan...  5.93 us

profile of v2, /device:TPU:0, one launch (start us, length us, event | category | flops | bytes accessed | tf_op | source)
XLA Modules:
  0.0 84.6 jit_solution(11438575389402332581)
XLA Ops:
  0.0 0.0 copy-start.3
  0.0 0.8 convert_bitcast_fusion
  0.8 0.7 pad_maximum_fusion.aux_ref
  1.5 5.9 %shard_map.73.proj_ref = bf16[512,256]{1,0:T(8,128)(2,1)} custom-call(bf16[64,576]{1,0:T(8,128)(2,1)} %weight_ref.1, bf16[1,576,2048]{2,1,0:T(8,128)(2,1)} %bank_ref.1), custom_call_target="tpu_custom_call" | custom-call | tf_op jit(solution)/shard_map/pallas_call | solution.py:31
  7.4 0.0 copy-done.3
  7.4 0.0 copy-start
  7.4 0.0 copy-start.1
  7.4 0.0 copy-start.2
  7.5 0.2 copy.19
  7.7 0.2 fusion
  7.9 0.2 copy.14
  8.1 0.1 copy.16.right_ref
  8.3 0.2 copy.13
  8.5 0.1 copy.15.left_ref
  8.6 0.1 copy-done
  8.7 0.0 copy-done.1
  8.7 0.0 copy-done.2
  8.7 34.7 %shard_map.74 = (bf16[2,512,256]{2,1,0:T(8,128)(2,1)S(1)}, bf16[16,64,128]{2,1,0:T(8,128)(2,1)S(1)}, bf16[16,64,128]{2,1,0:T(8,128)(2,1)S(1)}, bf16[8,64,128]{2,...) custom-call(s32[2]{0:T(128)S(1)} %copy-done.2, ...), custom_call_target="tpu_custom_call" | custom-call | tf_op jit(solution)/shard_map/pallas_call | solution.py:176
  43.5 40.0 %shard_map.75 = bf16[32,64,128]{2,1,0:T(8,128)(2,1)S(1)} custom-call(bf16[2,512,256]{2,1,0:T(8,128)(2,1)S(1)} %get-tuple-element.12.pages_ref, bf16[32,64,128]{2,1,0:T(8,128)(2,1)S(1)} %bitcast.17, bf16[16,64,128]{2,1,0:T(8,128)(2,1)S(1)} %get-tuple-element.13.above_ref, bf16[16,64,128]{2,1,0:T(8,128)(2,1)S(1)} %get-tuple-element.14.below_ref, ...), custom_call_target="tpu_custom_call" | custom-call | tf_op jit(solution)/shard_map/pallas_call | solution.py:311
  83.5 1.1 %copy.17 = bf16[64,32,128]{2,1,0:T(8,128)(2,1)} copy(bf16[64,32,128]{2,0,1:T(8,128)(2,1)S(1)} %bitcast.18) | data formatting | bytes 1048576 | tf_op jit(solution)/shard_map/transpose | solution.py:345
Async XLA Ops:
  0.0 7.4 %copy-start.3 = (bf16[64,32,128]{2,1,0:T(8,128)(2,1)S(1)}, bf16[64,32,128]{2,1,0:T(8,128)(2,1)}, u32[]{:S(2)}) copy-start(bf16[64,32,128]{2,1,0:T(8,128)(2,1)} %param.7) | copy-start | bytes 1572868
  7.4 1.3 %copy-start = (bf16[8,9,64,64]{3,2,1,0:T(8,128)(2,1)S(1)}, bf16[8,9,64,64]{3,2,1,0:T(8,128)(2,1)}, u32[]{:S(2)}) copy-start(bf16[8,9,64,64]{3,2,1,0:T(8,128)(2,1)} %taps_ref.1) | copy-start | bytes 1769476
  7.4 1.3 %copy-start.1 = (bf16[512,256]{1,0:T(8,128)(2,1)S(1)}, bf16[512,256]{1,0:T(8,128)(2,1)}, u32[]{:S(2)}) copy-start(bf16[512,256]{1,0:T(8,128)(2,1)} %shard_map.73.proj_ref) | copy-start | bytes 786436
  7.4 1.3 %copy-start.2 = (s32[2]{0:T(128)S(1)}, s32[2]{0:T(128)}, u32[]{:S(2)}) copy-start(s32[2]{0:T(128)} %owner_ref.1) | copy-start | bytes 28

commit v3 on v2

--- a/solution.py
+++ b/solution.py
@@ -20,9 +20,13 @@
 
 
 def project_kernel(weight_ref, bank_ref, out_ref):
-    out_ref[...] = jnp.dot(
-        weight_ref[...], bank_ref[0], preferred_element_type=jnp.float32
-    ).astype(jnp.bfloat16)
+    chans = weight_ref.shape[0]
+    for h in range(bank_ref.shape[2] // LOW):
+        out_ref[h * chans : (h + 1) * chans, :] = jnp.dot(
+            weight_ref[...],
+            bank_ref[0, :, h * LOW : (h + 1) * LOW],
+            preferred_element_type=jnp.float32,
+        ).astype(jnp.bfloat16)
 
 
 def project(texture_weight, bank):
@@ -30,12 +34,12 @@
     high = bank.shape[2] // LOW
     return pl.pallas_call(
         project_kernel,
-        grid=(high,),
+        grid=(2,),
         in_specs=[
             pl.BlockSpec((chans, depth), lambda h: (0, 0)),
-            pl.BlockSpec((1, depth, LOW), lambda h: (0, 0, h)),
+            pl.BlockSpec((1, depth, high // 2 * LOW), lambda h: (0, 0, h)),
         ],
-        out_specs=pl.BlockSpec((chans, LOW), lambda h: (h, 0)),
+        out_specs=pl.BlockSpec((high // 2 * chans, LOW), lambda h: (h, 0)),
         out_shape=jax.ShapeDtypeStruct((high * chans, LOW), jnp.bfloat16),
     )(texture_weight, bank)
 
@@ -259,11 +263,12 @@
 
     for ref, start, size in ((above_ref, 0, HALO), (state_ref, HALO, tile_h), (below_ref, HALO + tile_h, HALO)):
         def begin_group(g, carry, ref=ref, start=start):
-            for spot in range(per):
-                begin_row(ref, g * per + spot, start // per + g, spot, start + g * per + spot)
+            for spot in range(HALO):
+                at = g * HALO + spot
+                begin_row(ref, at, (start + g * HALO) // per + spot // per, spot % per, start + at)
             return carry
 
-        lax.fori_loop(0, size // per, begin_group, 0)
+        lax.fori_loop(0, size // HALO, begin_group, 0)
 
     for layer in range(STEPS * LAYERS):
         source, target = (field, inner) if layer % 2 == 0 else (inner, field)

time: 84.9 us -> 80.9 us (0.953)
  Pallas kernels: 80.6 us -> 76.6 us
    pallas_call x1, Pallas kernels: 5.93 us -> 2.65 us  [project(): pl.pallas_call(project_kernel, grid=(2,), in_specs=[pl.BlockSpec((chans,...]
where the time goes in v3:
time: 80.9 us; the launch traced here: 80.6 us
  Pallas kernels  76.6 us (95%)
  local copies, waits for them, and re-layouts  2.41 us (3%)
  other arithmetic  1.5 us (2%)
    pallas_call x1, Pallas kernels, trunk(): pl.pallas_call(functools.partial(trunk_kernel, rows, cols), in_specs=[VME...  39.3 us
    pallas_call x1, Pallas kernels, exchange(): pl.pallas_call(functools.partial(exchange_kernel, rows, cols, hubs), in_s...  34.7 us
    pallas_call x1, Pallas kernels, project(): pl.pallas_call(project_kernel, grid=(2,), in_specs=[pl.BlockSpec((chans,...  2.65 us

profile of v3, /device:TPU:0, one launch (start us, length us, event | category | flops | bytes accessed | tf_op | source)
XLA Modules:
  0.0 80.6 jit_solution(5932052414134113254)
XLA Ops:
  0.0 0.0 copy-start.3
  0.0 0.8 convert_bitcast_fusion
  0.8 0.7 pad_maximum_fusion.aux_ref
  1.5 2.6 %shard_map.73.proj_ref = bf16[512,256]{1,0:T(8,128)(2,1)} custom-call(bf16[64,576]{1,0:T(8,128)(2,1)} %weight_ref.1, bf16[1,576,2048]{2,1,0:T(8,128)(2,1)} %bank_ref.1), custom_call_target="tpu_custom_call" | custom-call | tf_op jit(solution)/shard_map/pallas_call | solution.py:35
  4.2 0.0 copy-done.3
  4.2 0.0 copy-start
  4.2 0.0 copy-start.1
  4.2 0.0 copy-start.2
  4.2 0.2 copy.19
  4.4 0.2 fusion
  4.6 0.2 copy.14
  4.9 0.1 copy.16.right_ref
  5.0 0.2 copy.13
  5.2 0.1 copy.15.left_ref
  5.3 0.1 copy-done
  5.4 0.0 copy-done.1
  5.5 0.0 copy-done.2
  5.5 34.7 %shard_map.74 = (bf16[2,512,256]{2,1,0:T(8,128)(2,1)S(1)}, bf16[16,64,128]{2,1,0:T(8,128)(2,1)S(1)}, bf16[16,64,128]{2,1,0:T(8,128)(2,1)S(1)}, bf16[8,64,128]{2,...) custom-call(s32[2]{0:T(128)S(1)} %copy-done.2, ...), custom_call_target="tpu_custom_call" | custom-call | tf_op jit(solution)/shard_map/pallas_call | solution.py:180
  40.2 39.3 %shard_map.75 = bf16[32,64,128]{2,1,0:T(8,128)(2,1)S(1)} custom-call(bf16[2,512,256]{2,1,0:T(8,128)(2,1)S(1)} %get-tuple-element.12.pages_ref, bf16[32,64,128]{2,1,0:T(8,128)(2,1)S(1)} %bitcast.17, bf16[16,64,128]{2,1,0:T(8,128)(2,1)S(1)} %get-tuple-element.13.above_ref, bf16[16,64,128]{2,1,0:T(8,128)(2,1)S(1)} %get-tuple-element.14.below_ref, ...), custom_call_target="tpu_custom_call" | custom-call | tf_op jit(solution)/shard_map/pallas_call | solution.py:316
  79.5 1.1 %copy.17 = bf16[64,32,128]{2,1,0:T(8,128)(2,1)} copy(bf16[64,32,128]{2,0,1:T(8,128)(2,1)S(1)} %bitcast.18) | data formatting | bytes 1048576 | tf_op jit(solution)/shard_map/transpose | solution.py:350
Async XLA Ops:
  0.0 4.2 %copy-start.3 = (bf16[64,32,128]{2,1,0:T(8,128)(2,1)S(1)}, bf16[64,32,128]{2,1,0:T(8,128)(2,1)}, u32[]{:S(2)}) copy-start(bf16[64,32,128]{2,1,0:T(8,128)(2,1)} %param.7) | copy-start | bytes 1572868
  4.2 1.3 %copy-start = (bf16[8,9,64,64]{3,2,1,0:T(8,128)(2,1)S(1)}, bf16[8,9,64,64]{3,2,1,0:T(8,128)(2,1)}, u32[]{:S(2)}) copy-start(bf16[8,9,64,64]{3,2,1,0:T(8,128)(2,1)} %taps_ref.1) | copy-start | bytes 1769476
  4.2 1.3 %copy-start.1 = (bf16[512,256]{1,0:T(8,128)(2,1)S(1)}, bf16[512,256]{1,0:T(8,128)(2,1)}, u32[]{:S(2)}) copy-start(bf16[512,256]{1,0:T(8,128)(2,1)} %shard_map.73.proj_ref) | copy-start | bytes 786436
  4.2 1.3 %copy-start.2 = (s32[2]{0:T(128)S(1)}, s32[2]{0:T(128)}, u32[]{:S(2)}) copy-start(s32[2]{0:T(128)} %owner_ref.1) | copy-start | bytes 28
